TPU v7x, 256 devices: a whole 4x4x8 slice. The times are simulated.
256 devices in a mesh: pair: 16 (over y, x_hi, core), virt: 16 (over z, x_lo).
Axes of the slice: x: 4 (x_hi: 2, x_lo: 2; x = x_hi * 2 + x_lo), y: 4, z: 8, core: 2. Of those that a mesh axis runs over, the one named last changes fastest.
Arguments:
- amplitudes: bfloat16 [256, 8, 128, 128], P('pair', None, 'virt'), may hold values from -6 to 6
- integrals: bfloat16 [96, 128, 8, 128, 128], P('pair', None, None, 'virt'), may hold values from -0.015625 to 0.015625
- pattern: int32 [8], replicated, may hold values from 0 to 7, as said below
- block_sizes: int32 [8], replicated, may hold values from 1 to 128, as said below
- pair_source: int32 [512], replicated, may hold values from 0 to 511, each once
Outputs:
- residual: float32 [512, 96, 128], P('pair', 'virt')
Inputs may be any that keep to these rules, and one draw needn't show every extreme that they name: pattern[pattern[C]] = C and pattern[C] != C. `block_sizes`: the sizes sum to 700.
All inputs are finite; a program needn't handle non-finite values.
Results may differ from a plain program's by a relative error of at most 0.0003.
Values may be sent and summed in bfloat16 or wider, within the bound.
A program may use at most 128 MiB of HBM per device.

v0:
```python
import jax
import jax.numpy as jnp
from jax import lax
from jax.sharding import PartitionSpec as P


def on_device(amplitudes, integrals, pattern, block_sizes, pair_source):
    stored, blocks, slice_rows, width = amplitudes.shape
    row_dev = integrals.shape[0]
    virt_count = lax.axis_size("virt")
    flat_len = blocks * slice_rows * width
    columns = lax.all_to_all(amplitudes, "virt", split_axis=3, concat_axis=2, tiled=True)
    flipped = jnp.swapaxes(jnp.take(columns, pattern, axis=1), 2, 3)
    generated = jnp.stack([amplitudes, flipped], axis=1).reshape(2 * stored, flat_len)
    everything = lax.all_gather(generated, "pair", axis=0, tiled=True)
    chosen = jnp.take(everything, pair_source, axis=0)
    slice_start = lax.axis_index("virt") * slice_rows
    own_slots = slice_start + jnp.arange(slice_rows, dtype=jnp.int32)
    row_live = own_slots[None, :] < block_sizes[:, None]
    all_slots = jnp.arange(width, dtype=jnp.int32)
    col_live = all_slots[None, :] < jnp.take(block_sizes, pattern)[:, None]
    live_mask = (
        (row_live[:, :, None] & col_live[:, None, :]).astype(jnp.bfloat16).reshape(1, flat_len)
    )
    chosen = chosen * live_mask
    slab = integrals.reshape(row_dev * width, flat_len)
    partial_value = lax.dot_general(
        chosen, slab, (((1,), (1,)), ((), ())), preferred_element_type=jnp.float32
    )
    partial_value = partial_value.reshape(chosen.shape[0], row_dev, width)
    total_rows = row_dev * lax.axis_size("pair")
    rows_mine = total_rows // virt_count
    summed = lax.psum(partial_value, "virt")
    routed = lax.all_to_all(summed, "pair", split_axis=0, concat_axis=1, tiled=True)
    mine = lax.dynamic_slice_in_dim(routed, lax.axis_index("virt") * rows_mine, rows_mine, 1)
    rows = lax.axis_index("virt") * rows_mine + jnp.arange(rows_mine, dtype=jnp.int32)
    row_blocks = rows % blocks
    offsets = rows // blocks
    a_live = offsets < jnp.take(block_sizes, row_blocks)
    b_live = all_slots[None, :] < jnp.take(block_sizes, jnp.take(pattern, row_blocks))[:, None]
    out_mask = (a_live[:, None] & b_live).astype(jnp.float32)
    return mine * out_mask[None]


def solution(mesh):
    return jax.shard_map(
        on_device,
        mesh=mesh,
        in_specs=(
            P("pair", None, "virt", None),
            P("pair", None, None, "virt", None),
            P(),
            P(),
            P(),
        ),
        out_specs=P("pair", "virt", None),
        check_vma=False,
    )
```

profile of v0, /device:TPU:28, one launch (start us, length us, event | category | flops | bytes accessed | tf_op | source)
XLA Modules:
  0.0 334.9 jit_solution(13421803159657510400)
XLA Ops:
  6.5 4.4 %copy.20 = bf16[16,8,8,128]{0,2,1,3:T(8,128)(2,1)S(1)} copy(bf16[16,8,8,128]{3,2,1,0:T(8,128)(2,1)} %param.7) | data formatting | bytes 524288 | tf_op args[0]
  11.0 2.8 reshape.187
  13.8 9.2 %all-to-all-start = ((bf16[16,2,4096]{2,1,0:T(2,128)(2,1)}), bf16[16,2,4096]{2,1,0:T(2,128)(2,1)S(1)}, u32[]{:S(2)}, u32[]{:S(2)}) async-start(bf16[16,2,4096]{2,1,0:T(2,128)(2,1)} %reshape.187), calls=%async_computation | async-start | bytes 524288 | tf_op jit(solution)/shard_map/all_to_all | solution.py:12
  23.0 0.0 all-gather.2.cloned.1.call-start
  23.0 1.0 copy.29
  24.0 0.7 compare_select_fusion.3
  24.7 1.3 gather_fusion.2
  26.0 0.7 broadcast_select_fusion
  26.7 8.4 %all-to-all-done = bf16[16,2,4096]{2,1,0:T(2,128)(2,1)S(1)} async-done(((bf16[16,2,4096]{2,1,0:T(2,128)(2,1)}), bf16[16,2,4096]{2,1,0:T(2,128)(2,1)S(1)}, u32[]{:S(2)}, u32[]{:S(2)}) %all-to-all-start) | async-done | bytes 262176 | tf_op jit(solution)/shard_map/all_to_all | solution.py:12
  35.0 1.4 reshape.188
  36.4 3.8 %copy.22 = bf16[16,8,16,8,8]{0,4,3,2,1:T(8,128)(2,1)} copy(bf16[16,8,16,8,8]{0,3,1,4,2:T(8,128)(2,1)S(1)} %bitcast.29) | data formatting | bytes 524288 | tf_op jit(solution)/shard_map/all_to_all | solution.py:12
  40.2 2.6 copy.23
  42.9 0.7 gather_fusion
  43.5 0.1 select_bitcast_fusion
  43.6 0.1 pad_maximum_fusion
  43.7 0.1 copy.24
  43.8 1.0 reshape.124
  44.8 0.0 all-gather.2.cloned.1.call-update
  44.9 0.2 all-reduce.2.cloned.1.call-start
  45.1 0.0 copy-start.2
  45.1 0.0 copy-start
  45.1 19.5 %dot_general.5 = bf16[6,128,8192]{2,1,0:T(8,128)(2,1)} reshape(bf16[6,128,8,8,128]{4,3,2,1,0:T(8,128)(2,1)} %param.8) | data formatting | bytes 25165824 | tf_op jit(solution)/shard_map/dot_general | solution.py:27
  64.6 0.0 copy-done.2
  64.6 0.1 iota_compare_fusion.1
  64.7 0.0 copy-done
  64.7 0.1 broadcast_compare_fusion
  64.8 0.1 fusion.7
  64.9 50.5 %all-gather.2.cloned.1.call-done = bf16[512,8192]{1,0:T(8,128)(2,1)} async-done(((bf16[32,8192]{1,0:T(8,128)(2,1)}), bf16[512,8192]{1,0:T(8,128)(2,1)}) %all-gather.2.cloned.1.call-update) | async-done | bytes 8388624 | tf_op jit(solution)/shard_map/all_gather | solution.py:15
  115.4 19.9 %gather_fusion.1 = bf16[512,8192]{1,0:T(8,128)(2,1)} fusion(bf16[512,8192]{1,0:T(8,128)(2,1)} %all-gather.2.cloned.1.call-done, s32[1024]{0:T(1024)S(1)} %pad_clamp_fusion.2), kind=kCustom, calls=%fused_computation.4 | custom fusion | bytes 16779264 | tf_op jit(solution)/shard_map/jit(_take)/gather | solution.py:16
  135.3 11.9 %fusion = f32[512,6,128]{2,0,1:T(8,128)} fusion(bf16[6,128,8192]{2,1,0:T(8,128)(2,1)} %dot_general.5, bf16[512,8192]{1,0:T(8,128)(2,1)} %gather_fusion.1, pred[512]{0:T(512)(128)(4,1)S(1)} %compare_and_fusion.2, bf16[8192]{0:T(1024)(128)(2,1)S(1)} %fusion.7), kind=kOutput, calls=%fused_computation.6 | convolution fusion | flops 6463422464 | bytes 22561280 | tf_op jit(solution)/shard_map/dot_general | solution.py:27
  147.2 0.0 copy-start.1
  147.2 0.0 all-reduce.2.cloned.1.call-update
  147.2 144.4 %all-reduce.2.cloned.1.call-done = f32[512,6,128]{2,0,1:T(8,128)} async-done(((f32[512,6,128]{2,0,1:T(8,128)}), f32[512,6,128]{2,0,1:T(8,128)}) %all-reduce.2.cloned.1.call-update) | async-done | bytes 1572880 | tf_op jit(solution)/shard_map/psum | solution.py:33
  291.6 3.7 %copy.25 = f32[512,6,128]{2,1,0:T(8,128)} copy(f32[512,6,128]{2,0,1:T(8,128)} %all-reduce.2.cloned.1.call-done) | data formatting | bytes 3145728 | tf_op jit(solution)/shard_map/psum | solution.py:33
  295.3 7.2 %all-to-all-start.1 = ((f32[512,6,128]{2,1,0:T(8,128)}), f32[512,6,128]{2,1,0:T(8,128)S(1)}, u32[]{:S(2)}, u32[]{:S(2)}) async-start(f32[512,6,128]{2,1,0:T(8,128)} %copy.25), calls=%async_computation.1 | async-start | bytes 4194304 | tf_op jit(solution)/shard_map/all_to_all | solution.py:34
  302.5 0.0 copy-done.1
  302.5 0.6 gather_fusion.4
  303.2 0.6 gather_fusion.3
  303.8 0.6 gather_fusion.5
  304.5 0.1 fusion.9
  304.6 22.5 %all-to-all-done.1 = f32[512,6,128]{2,1,0:T(8,128)S(1)} async-done(((f32[512,6,128]{2,1,0:T(8,128)}), f32[512,6,128]{2,1,0:T(8,128)S(1)}, u32[]{:S(2)}, u32[]{:S(2)}) %all-to-all-start.1) | async-done | bytes 1572896 | tf_op jit(solution)/shard_map/all_to_all | solution.py:34
  327.1 0.3 copy.26
  327.4 0.7 dynamic-slice_multiply_fusion
  (11 shorter events, 0.1 us)
Async XLA Ops:
  13.8 21.2 %all-to-all-start = ((bf16[16,2,4096]{2,1,0:T(2,128)(2,1)}), bf16[16,2,4096]{2,1,0:T(2,128)(2,1)S(1)}, u32[]{:S(2)}, u32[]{:S(2)}) async-start(bf16[16,2,4096]{2,1,0:T(2,128)(2,1)} %reshape.187), calls=%async_computation | async-start | bytes 524288 | tf_op jit(solution)/shard_map/all_to_all | solution.py:12
  23.0 92.4 %all-gather.2.cloned.1.call-start = ((), (), s32[]{:S(2)}) async-start(), calls=%async_computation.2 | async-start | bytes 8912896 | tf_op jit(solution)/shard_map/all_gather | solution.py:15
  44.9 246.8 %all-reduce.2.cloned.1.call-start = ((), (), s32[]{:S(2)}) async-start(), calls=%async_computation.3 | async-start | bytes 3145728 | tf_op jit(solution)/shard_map/psum | solution.py:33
  45.1 19.5 %copy-start.2 = (s32[512]{0:T(512)S(1)}, s32[512]{0:T(512)}, u32[]{:S(2)}) copy-start(s32[512]{0:T(512)} %param.11) | copy-start | bytes 6148
  45.1 19.6 %copy-start = (s32[8]{0:T(128)S(1)}, s32[8]{0:T(128)}, u32[]{:S(2)}) copy-start(s32[8]{0:T(128)} %param.10) | copy-start | bytes 100
  147.2 155.3 %copy-start.1 = (s32[8]{0:T(128)S(1)}, s32[8]{0:T(128)}, u32[]{:S(2)}) copy-start(s32[8]{0:T(128)} %param.9) | copy-start | bytes 100
  295.3 31.8 %all-to-all-start.1 = ((f32[512,6,128]{2,1,0:T(8,128)}), f32[512,6,128]{2,1,0:T(8,128)S(1)}, u32[]{:S(2)}, u32[]{:S(2)}) async-start(f32[512,6,128]{2,1,0:T(8,128)} %copy.25), calls=%async_computation.1 | async-start | bytes 4194304 | tf_op jit(solution)/shard_map/all_to_all | solution.py:34
Sparse Core Ops, SparseCore 0:
  45.0 70.3 all-gather.1
  147.4 144.2 all-reduce.1
where the time goes:
time: 341 us; the launch traced here: 335 us
  waiting for transfers between devices  226 us (66%)
  local copies, waits for them, and re-layouts  64.5 us (19%)
  starting transfers between devices  16.6 us (5%)
  between operations  13.6 us (4%)
  matrix products  11.9 us (3%)
    psum x1, waiting for transfers between devices, on_device(): summed = lax.psum(partial_value, 'virt')  144 us
    all_gather x1, waiting for transfers between devices, on_device(): everything = lax.all_gather(generated, 'pair', axis=0, tiled=True)  50.5 us
    all_to_all x1, waiting for transfers between devices, on_device(): lax.all_to_all(summed, 'pair', split_axis=0, concat_axis=1, tiled=True)  22.5 us
    gather x1, local copies, waits for them, and re-layouts, on_device(): chosen = jnp.take(everything, pair_source, axis=0)  19.9 us
    dot_general x1, local copies, waits for them, and re-layouts, on_device(): lax.dot_general(chosen, slab, (((1,), (1,)), ((), ())), preferred_element...  19.5 us
    dot_general x1, matrix products, on_device(): lax.dot_general(chosen, slab, (((1,), (1,)), ((), ())), preferred_element...  11.9 us
    unnamed x10, local copies, waits for them, and re-layouts  9.66 us
    all_to_all x1, starting transfers between devices, on_device(): lax.all_to_all(amplitudes, 'virt', split_axis=3, concat_axis=2, tiled=True)  9.2 us
  transfers between devices with their start and end apart: 4, of which 4 were waited for; matrix products, arithmetic and copies ran while one was open for 8% of the time, Pallas kernels for 0%

commit v1 on v0

v1 whole, which is shorter than its diff:
```python
import jax
import jax.numpy as jnp
from jax import lax
from jax.sharding import PartitionSpec as P


def on_device(amplitudes, integrals, pattern, block_sizes, pair_source):
    stored, blocks, slice_rows, width = amplitudes.shape
    row_dev = integrals.shape[0]
    virt_count = lax.axis_size("virt")
    flat_len = blocks * slice_rows * width
    columns = lax.all_to_all(amplitudes, "virt", split_axis=3, concat_axis=2, tiled=True)
    flipped = jnp.swapaxes(jnp.take(columns, pattern, axis=1), 2, 3)
    slice_start = lax.axis_index("virt") * slice_rows
    own_slots = slice_start + jnp.arange(slice_rows, dtype=jnp.int32)
    row_live = own_slots[None, :] < block_sizes[:, None]
    all_slots = jnp.arange(width, dtype=jnp.int32)
    col_live = all_slots[None, :] < jnp.take(block_sizes, pattern)[:, None]
    live_mask = (row_live[:, :, None] & col_live[:, None, :]).astype(jnp.bfloat16)
    generated = jnp.stack([amplitudes, flipped], axis=1) * live_mask[None, None]
    generated = generated.reshape(2 * stored, flat_len)
    everything = lax.all_gather(generated, "pair", axis=0, tiled=True)
    slab = integrals.reshape(row_dev * width, flat_len)
    partial_value = lax.dot_general(
        everything, slab, (((1,), (1,)), ((), ())), preferred_element_type=jnp.float32
    )
    partial_value = jnp.take(partial_value, pair_source, axis=0)
    mine = lax.psum_scatter(partial_value, "virt", scatter_dimension=0, tiled=True)
    count = virt_count
    perm = [(p * count + v, v * count + p) for p in range(count) for v in range(count)]
    mine = lax.ppermute(mine, ("pair", "virt"), perm)
    mine = mine.reshape(mine.shape[0], row_dev, width)
    rows = lax.axis_index("virt") * row_dev + jnp.arange(row_dev, dtype=jnp.int32)
    row_blocks = rows % blocks
    offsets = rows // blocks
    a_live = offsets < jnp.take(block_sizes, row_blocks)
    b_live = all_slots[None, :] < jnp.take(block_sizes, jnp.take(pattern, row_blocks))[:, None]
    out_mask = a_live[:, None] & b_live
    return jnp.where(out_mask[None], mine, 0.0)


def solution(mesh):
    return jax.shard_map(
        on_device,
        mesh=mesh,
        in_specs=(
            P("pair", None, "virt", None),
            P("pair", None, None, "virt", None),
            P(),
            P(),
            P(),
        ),
        out_specs=P("pair", "virt", None),
        check_vma=False,
    )
```

time: 341 us -> 230 us (0.67); the launches traced: 335 us -> 229 us
  waiting for transfers between devices: 226 us -> 148 us
  local copies, waits for them, and re-layouts: 64.5 us -> 40.7 us
  starting transfers between devices: 16.6 us -> 12.1 us
    psum x1 -> x0, waiting for transfers between devices: 144 us -> none  [on_device(): summed = lax.psum(partial_value, 'virt')]
    reduce_scatter x0 -> x1, waiting for transfers between devices: none -> 72.9 us  [on_device(): lax.psum_scatter(partial_value, 'virt', scatter_dimension=0, tiled=True)]
    all_to_all x1 -> x0, waiting for transfers between devices: 22.5 us -> none  [on_device(): lax.all_to_all(summed, 'pair', split_axis=0, concat_axis=1, tiled=True)]
    dot_general x1 -> x0, local copies, waits for them, and re-layouts: 19.5 us -> none  [on_device(): lax.dot_general(chosen, slab, (((1,), (1,)), ((), ())), preferred_element...]
    reshape x1 -> x2, local copies, waits for them, and re-layouts: 1.03 us -> 19.4 us  [the longest x1 19.4 us: on_device(): slab = integrals.reshape(row_dev * width, flat_len)]
    gather x1, local copies, waits for them, and re-layouts: 19.9 us -> 1.89 us  [on_device(): partial_value = jnp.take(partial_value, pair_source, axis=0)]
    ppermute x0 -> x1, waiting for transfers between devices: none -> 13.1 us  [on_device(): mine = lax.ppermute(mine, ('pair', 'virt'), perm)]
    all_to_all x1 -> x0, starting transfers between devices: 7.17 us -> none  [on_device(): lax.all_to_all(summed, 'pair', split_axis=0, concat_axis=1, tiled=True)]
  transfers between devices with their start and end apart: 4 -> 4, of which waited for: 4 -> 4; matrix products, arithmetic and copies ran while one was open for 8% -> 10% of each run, Pallas kernels for 0% -> 0%
where the time goes in v1:
time: 230 us; the launch traced here: 229 us
  waiting for transfers between devices  148 us (64%)
  local copies, waits for them, and re-layouts  40.7 us (18%)
  between operations  13.6 us (6%)
  starting transfers between devices  12.1 us (5%)
  matrix products  11.9 us (5%)
  other arithmetic  2.75 us (1%)
    reduce_scatter x1, waiting for transfers between devices, on_device(): lax.psum_scatter(partial_value, 'virt', scatter_dimension=0, tiled=True)  72.9 us
    all_gather x1, waiting for transfers between devices, on_device(): everything = lax.all_gather(generated, 'pair', axis=0, tiled=True)  51 us
    reshape x1, local copies, waits for them, and re-layouts, on_device(): slab = integrals.reshape(row_dev * width, flat_len)  19.4 us
    ppermute x1, waiting for transfers between devices, on_device(): mine = lax.ppermute(mine, ('pair', 'virt'), perm)  13.1 us
    dot_general x1, matrix products, on_device(): lax.dot_general(everything, slab, (((1,), (1,)), ((), ())), preferred_ele...  11.9 us
    all_to_all x1, waiting for transfers between devices, on_device(): lax.all_to_all(amplitudes, 'virt', split_axis=3, concat_axis=2, tiled=True)  11 us
    all_to_all x1, starting transfers between devices, on_device(): lax.all_to_all(amplitudes, 'virt', split_axis=3, concat_axis=2, tiled=True)  9.2 us
    unnamed x12, local copies, waits for them, and re-layouts  8.77 us
  transfers between devices with their start and end apart: 4, of which 4 were waited for; matrix products, arithmetic and copies ran while one was open for 10% of the time, Pallas kernels for 0%

profile of v1, /device:TPU:28, one launch (start us, length us, event | category | flops | bytes accessed | tf_op | source)
XLA Modules:
  0.0 229.1 jit_solution(1371521087622127316)
XLA Ops:
  6.5 0.0 copy-start.1
  6.5 0.0 copy-start
  6.5 4.5 %copy.14 = bf16[16,8,8,128]{0,2,1,3:T(8,128)(2,1)S(1)} copy(bf16[16,8,8,128]{3,2,1,0:T(8,128)(2,1)} %param.7) | data formatting | bytes 524288 | tf_op args[0]
  11.0 0.0 copy-start.2
  11.0 2.8 %reshape.178 = bf16[16,2,4096]{2,1,0:T(2,128)(2,1)} reshape(bf16[128,8,8,16]{3,2,1,0:T(8,128)(2,1)S(1)} %bitcast.21) | data formatting | bytes 524288
  13.8 9.2 %all-to-all-start = ((bf16[16,2,4096]{2,1,0:T(2,128)(2,1)}), bf16[16,2,4096]{2,1,0:T(2,128)(2,1)S(1)}, u32[]{:S(2)}, u32[]{:S(2)}) async-start(bf16[16,2,4096]{2,1,0:T(2,128)(2,1)} %reshape.178), calls=%async_computation | async-start | bytes 524288 | tf_op jit(solution)/shard_map/all_to_all | solution.py:12
  23.0 0.0 all-gather.2.cloned.1.call-start
  23.1 0.0 copy-done.1
  23.1 0.0 copy-done
  23.1 0.6 gather_fusion.1
  23.8 0.1 iota_compare_fusion
  23.9 0.0 copy-done.2
  23.9 0.1 copy.22
  23.9 0.1 broadcast_compare_fusion
  24.0 0.1 fusion
  24.1 11.0 %all-to-all-done = bf16[16,2,4096]{2,1,0:T(2,128)(2,1)S(1)} async-done(((bf16[16,2,4096]{2,1,0:T(2,128)(2,1)}), bf16[16,2,4096]{2,1,0:T(2,128)(2,1)S(1)}, u32[]{:S(2)}, u32[]{:S(2)}) %all-to-all-start) | async-done | bytes 262176 | tf_op jit(solution)/shard_map/all_to_all | solution.py:12
  35.1 1.4 reshape.179
  36.5 3.8 %copy.16 = bf16[16,8,16,8,8]{0,4,3,2,1:T(8,128)(2,1)} copy(bf16[16,8,16,8,8]{0,3,1,4,2:T(8,128)(2,1)S(1)} %bitcast.22) | data formatting | bytes 524288 | tf_op jit(solution)/shard_map/all_to_all | solution.py:12
  40.3 2.6 %copy.17 = bf16[16,8,128,8]{2,3,1,0:T(8,128)(2,1)S(1)} copy(bf16[16,8,128,8]{0,3,2,1:T(8,128)(2,1)} %bitcast.23) | data formatting | bytes 524288 | tf_op jit(solution)/shard_map/all_to_all | solution.py:12
  42.9 0.7 gather_fusion
  43.6 0.1 select_bitcast_fusion
  43.7 0.1 pad_maximum_fusion
  43.7 0.1 copy.18
  43.9 0.2 stack.14
  44.1 0.8 broadcast_multiply_fusion
  45.0 0.0 all-gather.2.cloned.1.call-update
  45.0 0.0 copy-start.3
  45.0 0.0 reduce-scatter.2.cloned.1.call-start
  45.0 19.4 %reshape.115 = bf16[768,8192]{1,0:T(8,128)(2,1)} reshape(bf16[6,128,8,8,128]{4,3,2,1,0:T(8,128)(2,1)} %param.8) | data formatting | bytes 25165824 | tf_op jit(solution)/shard_map/reshape | solution.py:23
  64.5 0.0 copy-done.3
  64.5 51.0 %all-gather.2.cloned.1.call-done = bf16[512,8192]{1,0:T(8,128)(2,1)} async-done(((bf16[32,8192]{1,0:T(8,128)(2,1)}), bf16[512,8192]{1,0:T(8,128)(2,1)}) %all-gather.2.cloned.1.call-update) | async-done | bytes 8388624 | tf_op jit(solution)/shard_map/all_gather | solution.py:22
  115.5 11.9 %fusion.2 = f32[512,768]{1,0:T(8,128)S(1)} fusion(bf16[512,8192]{1,0:T(8,128)(2,1)} %all-gather.2.cloned.1.call-done, bf16[768,8192]{1,0:T(8,128)(2,1)} %reshape.115), kind=kOutput, calls=%fused_computation.39 | convolution fusion | flops 6442450944 | bytes 22544384 | tf_op jit(solution)/shard_map/dot_general | solution.py:24
  127.4 1.9 gather_fusion.2
  129.3 1.3 broadcast_select_fusion
  130.6 0.0 reduce-scatter.2.cloned.1.call-update
  130.7 0.6 gather_fusion.4
  131.3 0.6 gather_fusion.3
  132.0 0.6 gather_fusion.5
  132.7 72.9 %reduce-scatter.2.cloned.1.call-done = f32[32,768]{1,0:T(8,128)} async-done(((f32[512,768]{1,0:T(8,128)}), f32[32,768]{1,0:T(8,128)}) %reduce-scatter.2.cloned.1.call-update) | async-done | bytes 98320 | tf_op jit(solution)/shard_map/reduce_scatter | solution.py:28
  205.6 2.9 %collective-permute-start = (f32[32,768]{1,0:T(8,128)}, f32[32,768]{1,0:T(8,128)S(1)}, u32[]{:S(2)}, u32[]{:S(2)}) collective-permute-start(f32[32,768]{1,0:T(8,128)} %reduce-scatter.2.cloned.1.call-done), channel_id=1, source_target_pairs={{0,0},{1,16},{2,32},{3,48},{4,64},{5,80},{6,96},{7,112},{8,128},{9... | collective-permute-start | bytes 294920 | tf_op jit(solution)/shard_map/ppermute | solution.py:31
  208.5 0.1 fusion.1
  208.5 13.1 %collective-permute-done = f32[32,768]{1,0:T(8,128)S(1)} collective-permute-done((f32[32,768]{1,0:T(8,128)}, f32[32,768]{1,0:T(8,128)S(1)}, u32[]{:S(2)}, u32[]{:S(2)}) %collective-permute-start) | collective-permute-done | bytes 98336 | tf_op jit(solution)/shard_map/ppermute | solution.py:31
  221.6 0.7 copy.19
  (15 shorter events, 0.1 us)
Async XLA Ops:
  6.5 16.6 %copy-start.1 = (s32[8]{0:T(128)S(1)}, s32[8]{0:T(128)}, u32[]{:S(2)}) copy-start(s32[8]{0:T(128)} %param.9) | copy-start | bytes 100
  6.5 16.6 %copy-start = (s32[8]{0:T(128)S(1)}, s32[8]{0:T(128)}, u32[]{:S(2)}) copy-start(s32[8]{0:T(128)} %param.10) | copy-start | bytes 100
  11.0 12.9 %copy-start.2 = (bf16[16,8,8,128]{3,2,1,0:T(8,128)(2,1)S(1)}, bf16[16,8,8,128]{3,2,1,0:T(8,128)(2,1)}, u32[]{:S(2)}) copy-start(bf16[16,8,8,128]{3,2,1,0:T(8,128)(2,1)} %param.7) | copy-start | bytes 786436
  13.8 21.2 %all-to-all-start = ((bf16[16,2,4096]{2,1,0:T(2,128)(2,1)}), bf16[16,2,4096]{2,1,0:T(2,128)(2,1)S(1)}, u32[]{:S(2)}, u32[]{:S(2)}) async-start(bf16[16,2,4096]{2,1,0:T(2,128)(2,1)} %reshape.178), calls=%async_computation | async-start | bytes 524288 | tf_op jit(solution)/shard_map/all_to_all | solution.py:12
  23.0 92.4 %all-gather.2.cloned.1.call-start = ((), (), s32[]{:S(2)}) async-start(), calls=%async_computation.2 | async-start | bytes 8912896 | tf_op jit(solution)/shard_map/all_gather | solution.py:22
  45.0 19.5 %copy-start.3 = (s32[512]{0:T(512)S(1)}, s32[512]{0:T(512)}, u32[]{:S(2)}) copy-start(s32[512]{0:T(512)} %param.11) | copy-start | bytes 6148
  45.0 160.6 %reduce-scatter.2.cloned.1.call-start = ((), (), s32[]{:S(2)}) async-start(), calls=%async_computation.3 | async-start | bytes 1671168 | tf_op jit(solution)/shard_map/reduce_scatter | solution.py:28
  205.6 16.0 %collective-permute-start = (f32[32,768]{1,0:T(8,128)}, f32[32,768]{1,0:T(8,128)S(1)}, u32[]{:S(2)}, u32[]{:S(2)}) collective-permute-start(f32[32,768]{1,0:T(8,128)} %reduce-scatter.2.cloned.1.call-done), channel_id=1, source_target_pairs={{0,0},{1,16},{2,32},{3,48},{4,64},{5,80},{6,96},{7,112},{8,128},{9... | collective-permute-start | bytes 294920 | tf_op jit(solution)/shard_map/ppermute | solution.py:31
Sparse Core Ops, SparseCore 0:
  45.1 70.3 all-gather.1
  130.8 74.7 reduce-scatter.1

commit v2 on v1

v2 whole, which is shorter than its diff:
```python
import functools

import jax
import jax.numpy as jnp
from jax import lax
from jax.experimental import pallas as pl
from jax.experimental.pallas import tpu as pltpu
from jax.sharding import PartitionSpec as P

MESH = pl.DeviceIdType.MESH
BF, F32 = jnp.bfloat16, jnp.float32
NB, SL, BW = 8, 8, 128
QS, PD, RD = 16, 32, 6
RB = RD * BW
CHUNK = 64
KP = 2 * NB * BW
FAR = (4, 3, 5, 2, 6, 1, 7)


def ladder_kernel(amp, integrals, pattern, sizes, source, out, slab, wide, basis, gathered, total, ordered, from_x, from_z, pieces,
                  staged, mixed, sent, landed, turned, summed, final,
                  slab_sem, a2a_send, a2a_recv, gat_send, gat_recv, x_send, x_recv, z_send, z_recv, fin_send, fin_recv):
    p, v = lax.axis_index("pair"), lax.axis_index("virt")
    y, h, core = p // 4, (p // 2) % 2, p % 2
    z, xl = v // 2, v % 2

    def pair_of(dy, dh, dc):
        return (((y + dy) % 4) * 2 + (h + dh) % 2) * 2 + (core + dc) % 2

    up, down, across, sibling = pair_of(1, 0, 0), pair_of(3, 0, 0), pair_of(0, 1, 0), pair_of(0, 0, 1)

    loads = []
    for k in range(RB // CHUNK):
        rows = pl.ds(k * CHUNK * NB * SL, CHUNK * NB * SL)
        load = pltpu.make_async_copy(integrals.at[rows], slab.at[rows], slab_sem.at[k])
        load.start()
        loads.append(load)

    barrier = pltpu.get_barrier_semaphore()
    for q in (up, down, across, sibling):
        pl.semaphore_signal(barrier, inc=1, device_id=(q, v), device_id_type=MESH)
    for j in range(1, 16):
        pl.semaphore_signal(barrier, inc=1, device_id=(p, (v + j) % 16), device_id_type=MESH)

    @pl.when(p != v)
    def _():
        pl.semaphore_signal(barrier, inc=1, device_id=(v, p), device_id_type=MESH)
        pl.semaphore_wait(barrier, 20)

    @pl.when(p == v)
    def _():
        pl.semaphore_wait(barrier, 19)

    lane = lax.broadcasted_iota(jnp.int32, (1, BW), 1)

    def mate_size(block):
        mate, partner = pattern[block], 0
        for other in range(NB):
            partner = jnp.where(mate == other, sizes[other], partner)
        return partner

    mate_sizes = [mate_size(block) for block in range(NB)]

    def live(block, offset):
        return lane < jnp.where(v * SL + offset < sizes[block], mate_sizes[block], 0)

    gat_sends = []

    def send(f, half, owner, q, index):
        part = pl.ds(half * 2, 2)
        copy = pltpu.make_async_remote_copy(
            src_ref=gathered.at[f, owner, part], dst_ref=gathered.at[f, owner, part],
            send_sem=gat_send.at[f, half, index], recv_sem=gat_recv.at[f, half, owner],
            device_id=(q, v), device_id_type=MESH)
        copy.start()
        gat_sends.append(copy)

    def arrived(f, half, owner):
        part = pl.ds(half * 2, 2)
        pltpu.make_async_remote_copy(
            src_ref=gathered.at[f, owner, part], dst_ref=gathered.at[f, owner, part],
            send_sem=gat_send.at[f, half, 0], recv_sem=gat_recv.at[f, half, owner],
            device_id=(p, v), device_id_type=MESH).wait_recv()

    def send_own(f):
        for half in range(2):
            for index, q in enumerate((up, down, across, sibling)):
                send(f, half, p, q, index)

    staged[...] = amp[...].astype(F32)
    for c in range(SL):
        for block in range(NB):
            piece = staged[pl.ds(block * SL + c, QS, stride=NB * SL), :]
            piece = jnp.where(live(block, c), piece, 0.0).astype(BF)
            lanes = pl.ds((c % 2) * NB * BW + block * BW, BW)
            gathered[0, p, c // 2, :, lanes] = piece
    send_own(0)

    group = lax.broadcasted_iota(jnp.int32, (SL, BW), 1) // SL

    def mix(block, carry):
        tiles = [staged[pl.ds(pl.multiple_of(q * NB * SL + block * SL, SL), SL), :] for q in range(QS)]
        for k in range(4):
            bit = 1 << k
            high = (group // bit) % 2 == 1
            new = list(tiles)
            for q in range(QS):
                if q & bit == 0:
                    new[q] = jnp.where(high, pltpu.roll(tiles[q | bit], SL * bit, 1), tiles[q])
                    new[q | bit] = jnp.where(high, tiles[q | bit], pltpu.roll(tiles[q], BW - SL * bit, 1))
            tiles = new
        for u in range(16):
            mixed[u, pl.ds(pl.multiple_of(block * SL, SL), SL), :] = tiles[u]
        return carry

    lax.fori_loop(0, NB, mix, 0)
    sent[...] = mixed[...].astype(BF)
    a2a = []
    for j in range(1, 16):
        u = (v + j) % 16
        copy = pltpu.make_async_remote_copy(
            src_ref=sent.at[u], dst_ref=landed.at[v], send_sem=a2a_send.at[j], recv_sem=a2a_recv.at[j],
            device_id=(p, u), device_id_type=MESH)
        copy.start()
        a2a.append(copy)
    landed[v] = sent[v]

    def relayout(k):
        rows = CHUNK * NB * SL
        wide[...] = slab[pl.ds(k * rows, rows), :].astype(F32)
        for c in range(SL):
            for block in range(NB):
                piece = wide[pl.ds(block * SL + c, CHUNK, stride=NB * SL), :].astype(BF)
                lanes = pl.ds((c % 2) * NB * BW + block * BW, BW)
                basis[c // 2, pl.ds(pl.multiple_of(k * CHUNK, CHUNK), CHUNK), lanes] = piece

    def relayouts(first, count):
        for k in range(first, first + count):
            loads[k].wait()

        def step(k, carry):
            relayout(k)
            return carry

        lax.fori_loop(first, first + count, step, 0)

    def event(f, half, kind):
        if kind == 0:
            owner, onward = pair_of(3, 0, 0), [(up, 4)] if half == 0 else []
        elif kind == 1:
            owner, onward = pair_of(1, 0, 0), [(down, 4)] if half == 1 else []
        elif kind == 2:
            owner, onward = across, [(up, 5), (down, 6)]
        elif kind == 3:
            owner, onward = pair_of(2, 0, 0), [(across, 7)]
        else:
            owner, onward = pair_of((3, 1, 2)[kind - 4], 1, 0), []
        arrived(f, half, owner)
        for q, index in onward:
            send(f, half, owner, q, index)
        send(f, half, owner, sibling, 8 + kind)

    def events(f, half, kinds):
        for kind in kinds:
            event(f, half, kind)

    def siblings(f, half):
        for dy in range(4):
            for dh in range(2):
                arrived(f, half, pair_of(dy, dh, 1))

    def multiply(f, half):
        rows = pl.ds(f * 256, 256)

        def step(c, carry):
            left = gathered[f, :, c].reshape(256, KP)
            part = lax.dot_general(left, basis[c], (((1,), (1,)), ((), ())), preferred_element_type=F32)
            total[rows, :] = total[rows, :] + part
            return carry

        lax.fori_loop(half * 2, half * 2 + 2, step, 0)

    relayouts(0, 2)
    events(0, 0, (0, 1, 2))
    relayouts(2, 2)
    events(0, 1, (0, 1, 2))

    for copy in a2a:
        copy.wait()
    mixed[...] = landed[...].astype(F32)
    for block in range(NB):
        mate = pattern[block]
        tile = mixed[:, pl.ds(0, SL), :]
        for other in range(1, NB):
            tile = jnp.where(mate == other, mixed[:, pl.ds(other * SL, SL), :], tile)
        turned[...] = tile.reshape(BW, BW).T
        for c in range(SL):
            piece = turned[pl.ds(c, QS, stride=SL), :]
            piece = jnp.where(live(block, c), piece, 0.0).astype(BF)
            lanes = pl.ds((c % 2) * NB * BW + block * BW, BW)
            gathered[1, p, c // 2, :, lanes] = piece
    send_own(1)

    total[...] = jnp.zeros_like(total)
    relayouts(4, 2)
    events(0, 0, (3, 4, 5, 6))
    relayouts(6, 2)
    events(0, 1, (3, 4, 5, 6))
    relayouts(8, 2)
    events(1, 0, (0, 1, 2))
    relayouts(10, 2)
    siblings(0, 0)
    events(1, 1, (0, 1, 2))
    multiply(0, 0)
    events(1, 0, (3, 4, 5, 6))
    siblings(0, 1)
    multiply(0, 1)
    events(1, 1, (3, 4, 5, 6))
    siblings(1, 0)
    multiply(1, 0)
    siblings(1, 1)
    multiply(1, 1)

    for part in range(4):
        rows = pl.ds(part * 128, 128)
        whole = total[rows, :]
        high = whole.astype(BF)
        rest = whole - high.astype(F32)
        middle = rest.astype(BF)
        pieces[0, rows, :] = high
        pieces[1, rows, :] = middle
        pieces[2, rows, :] = (rest - middle.astype(F32)).astype(BF)
    generated = lax.broadcasted_iota(jnp.int32, (PD, 512), 1)

    def reorder(owners):
        takes = []
        for owner in owners:
            g = source[pl.ds(pl.multiple_of(owner * PD, PD), PD), :]
            takes.append(jnp.where(generated == (g & 1) * 256 + (g >> 1), 1.0, 0.0))
        take = jnp.concatenate(takes, axis=0).astype(BF)
        rows = lax.dot_general(take, pieces[0], (((1,), (0,)), ((), ())), preferred_element_type=F32)
        for k in (1, 2):
            rows += lax.dot_general(take, pieces[k], (((1,), (0,)), ((), ())), preferred_element_type=F32)
        for j, owner in enumerate(owners):
            ordered[owner] = rows[j * PD:(j + 1) * PD]

    order = [(z + dz) % 8 for dz in FAR + (0,)]
    x_copies = []
    for part in (0, 4):
        reorder([u * 2 + 1 - xl for u in order[part:part + 4]])
        for j in range(part, part + 4):
            copy = pltpu.make_async_remote_copy(
                src_ref=ordered.at[order[j] * 2 + 1 - xl], dst_ref=from_x.at[j], send_sem=x_send.at[j],
                recv_sem=x_recv.at[j], device_id=(p, z * 2 + 1 - xl), device_id_type=MESH)
            copy.start()
            x_copies.append(copy)
    for part in (0, 4):
        reorder([u * 2 + xl for u in order[part:part + 4]])
    z_copies = []
    for j, dz in enumerate(FAR + (0,)):
        owner = ((z + dz) % 8) * 2 + xl
        x_copies[j].wait_recv()
        ordered[owner] = ordered[owner] + from_x[j]
        if dz:
            copy = pltpu.make_async_remote_copy(
                src_ref=ordered.at[owner], dst_ref=from_z.at[j], send_sem=z_send.at[j], recv_sem=z_recv.at[j],
                device_id=(p, owner), device_id_type=MESH)
            copy.start()
            z_copies.append(copy)
    acc = ordered[v]
    for j, copy in enumerate(z_copies):
        copy.wait_recv()
        acc = acc + from_z[j]
    summed[...] = acc

    @pl.when(p == v)
    def _():
        final[...] = summed[...]

    @pl.when(p != v)
    def _():
        copy = pltpu.make_async_remote_copy(
            src_ref=summed, dst_ref=final, send_sem=fin_send, recv_sem=fin_recv, device_id=(v, p), device_id_type=MESH)
        copy.start()
        copy.wait()

    for i in range(RD):
        row = v * RD + i
        width = 0
        for block in range(NB):
            here = jnp.where(row // NB < sizes[block], mate_sizes[block], 0)
            width = jnp.where(row % NB == block, here, width)
        lanes = pl.ds(i * BW, BW)
        out[:, lanes] = jnp.where(lane < width, final[:, lanes], 0.0)
    for copy in gat_sends + x_copies + z_copies:
        copy.wait_send()


def on_device(amplitudes, integrals, pattern, block_sizes, pair_source):
    vmem, smem = pl.BlockSpec(memory_space=pltpu.VMEM), pl.BlockSpec(memory_space=pltpu.SMEM)
    dma = pltpu.SemaphoreType.DMA
    result = pl.pallas_call(
        ladder_kernel,
        out_shape=jax.ShapeDtypeStruct((PD, RB), F32),
        in_specs=[vmem, pl.BlockSpec(memory_space=pl.ANY), smem, smem, vmem],
        out_specs=vmem,
        scratch_shapes=[
            pltpu.VMEM((RB * NB * SL, BW), BF),
            pltpu.VMEM((CHUNK * NB * SL, BW), F32),
            pltpu.VMEM((4, RB, KP), BF),
            pltpu.VMEM((2, 16, 4, QS, KP), BF),
            pltpu.VMEM((512, RB), F32),
            pltpu.VMEM((16, PD, RB), F32),
            pltpu.VMEM((8, PD, RB), F32),
            pltpu.VMEM((7, PD, RB), F32),
            pltpu.VMEM((3, 512, RB), BF),
            pltpu.VMEM((QS * NB * SL, BW), F32),
            pltpu.VMEM((16, NB * SL, BW), F32),
            pltpu.VMEM((16, NB * SL, BW), BF),
            pltpu.VMEM((16, NB * SL, BW), BF),
            pltpu.VMEM((BW, BW), F32),
            pltpu.VMEM((PD, RB), F32),
            pltpu.VMEM((PD, RB), F32),
            dma((RB // CHUNK,)),
            dma((16,)), dma((16,)),
            dma((2, 2, 16)), dma((2, 2, 16)),
            dma((8,)), dma((8,)), dma((7,)), dma((7,)),
            dma, dma,
        ],
        compiler_params=pltpu.CompilerParams(collective_id=0, has_side_effects=True, vmem_limit_bytes=60 * 2**20),
        cost_estimate=pl.CostEstimate(flops=2 * 512 * RB * 8192, bytes_accessed=14 * 2**20, transcendentals=0),
    )(amplitudes.reshape(QS * NB * SL, BW), integrals.reshape(RB * NB * SL, BW), pattern, block_sizes, pair_source.reshape(512, 1))
    return result.reshape(PD, RD, BW)


def solution(mesh):
    return jax.shard_map(
        on_device,
        mesh=mesh,
        in_specs=(P("pair", None, "virt", None), P("pair", None, None, "virt", None), P(), P(), P()),
        out_specs=P("pair", "virt", None),
        check_vma=False,
    )
```

time: 230 us -> 107 us (0.47)
  waiting for transfers between devices: 148 us -> 0 us
  Pallas kernels: 0 us -> 103 us
  local copies, waits for them, and re-layouts: 40.7 us -> 3.06 us
  between operations: 13.6 us -> 0.01 us
  starting transfers between devices: 12.1 us -> 0 us
  matrix products: 11.9 us -> 0 us
  other arithmetic: 2.75 us -> 0 us
    pallas_call x0 -> x1, Pallas kernels: none -> 103 us  [on_device(): pl.pallas_call(ladder_kernel, out_shape=jax.ShapeDtypeStruct((PD, RB), F3...]
    reduce_scatter x1 -> x0, waiting for transfers between devices: 72.9 us -> none  [on_device(): lax.psum_scatter(partial_value, 'virt', scatter_dimension=0, tiled=True)]
    all_gather x1 -> x0, waiting for transfers between devices: 51 us -> none  [on_device(): everything = lax.all_gather(generated, 'pair', axis=0, tiled=True)]
    reshape x2, local copies, waits for them, and re-layouts: 19.4 us -> 3.06 us  [the longest x1 1.54 us: on_device(): return result.reshape(PD, RD, BW)]
    ppermute x1 -> x0, waiting for transfers between devices: 13.1 us -> none  [on_device(): mine = lax.ppermute(mine, ('pair', 'virt'), perm)]
    dot_general x1 -> x0, matrix products: 11.9 us -> none  [on_device(): lax.dot_general(everything, slab, (((1,), (1,)), ((), ())), preferred_ele...]
    all_to_all x1 -> x0, waiting for transfers between devices: 11 us -> none  [on_device(): lax.all_to_all(amplitudes, 'virt', split_axis=3, concat_axis=2, tiled=True)]
    all_to_all x1 -> x0, starting transfers between devices: 9.2 us -> none  [on_device(): lax.all_to_all(amplitudes, 'virt', split_axis=3, concat_axis=2, tiled=True)]
  transfers between devices with their start and end apart: 4 -> 0, of which waited for: 4 -> 0; matrix products, arithmetic and copies ran while one was open for 10% -> 0% of each run, Pallas kernels for 0% -> 0%
where the time goes in v2:
time: 107 us; the launch traced here: 106 us
  Pallas kernels  103 us (96%)
  local copies, waits for them, and re-layouts  3.06 us (3%)
    pallas_call x1, Pallas kernels, on_device(): pl.pallas_call(ladder_kernel, out_shape=jax.ShapeDtypeStruct((PD, RB), F3...  103 us

profile of v2, /device:TPU:28, one launch (start us, length us, event | category | flops | bytes accessed | tf_op | source)
XLA Modules:
  0.0 106.2 jit_solution(13866219881132465885)
XLA Ops:
  0.0 1.5 %copy.7.source = s32[512,1]{1,0:T(8,128)} copy(s32[512,1]{0,1:T(1,128)} %bitcast.8) | data formatting | bytes 4096 | tf_op jit(solution)/shard_map/reshape | solution.py:332
  1.5 103.1 %shard_map.55 = f32[32,768]{1,0:T(8,128)} custom-call(bf16[1024,128]{1,0:T(8,128)(2,1)} %bitcast.10, bf16[49152,128]{1,0:T(8,128)(2,1)} %bitcast.9, s32[8]{0:T(128)} %pattern.1, s32[8]{0:T(128)} %sizes.1, s32[512,1]{1,0:T(8,128)} %copy.7.source), custom_call_target="tpu_custom_call" | custom-call | flops 6442450944 | bytes 14680064 | tf_op jit(solution)/shard_map/pallas_call | solution.py:302
  104.6 1.5 %copy_bitcast_fusion = f32[32,6,128]{2,0,1:T(8,128)} fusion(f32[32,768]{1,0:T(8,128)} %shard_map.55), kind=kLoop, calls=%fused_computation | loop fusion | bytes 196608 | tf_op jit(solution)/shard_map/reshape | solution.py:333

commit v3 on v2

v3 whole, which is shorter than its diff:
```python
import functools

import jax
import jax.numpy as jnp
from jax import lax
from jax.experimental import pallas as pl
from jax.experimental.pallas import tpu as pltpu
from jax.sharding import PartitionSpec as P

MESH = pl.DeviceIdType.MESH
BF, F32 = jnp.bfloat16, jnp.float32
NB, SL, BW = 8, 8, 128
QS, PD, RD = 16, 32, 6
RB = RD * BW
CHUNK = 128
LANES = NB * BW
KP = 1408
WIN = 768
REACH = (((0, 6), (2, 8), (4, 8)), ((0, 6), (0, 8), (2, 8)))
FAR = (4, 3, 5, 2, 6, 1, 7)


def ladder_kernel(amp, integrals, pattern, sizes, source, out, slab, narrow, select, few, basis, gathered, total, ordered, from_x, from_z, pieces,
                  staged, mixed, sent, landed, turned, column, summed, final,
                  slab_sem, a2a_send, a2a_recv, gat_send, gat_recv, x_send, x_recv, z_send, z_recv, fin_send, fin_recv):
    p, v = lax.axis_index("pair"), lax.axis_index("virt")
    y, h, core = p // 4, (p // 2) % 2, p % 2
    z, xl = v // 2, v % 2

    def pair_of(dy, dh, dc):
        return (((y + dy) % 4) * 2 + (h + dh) % 2) * 2 + (core + dc) % 2

    up, down, across, sibling = pair_of(1, 0, 0), pair_of(3, 0, 0), pair_of(0, 1, 0), pair_of(0, 0, 1)

    def load(k):
        rows = pl.ds(pl.multiple_of(k * CHUNK * NB * SL, CHUNK * NB * SL), CHUNK * NB * SL)
        return pltpu.make_async_copy(integrals.at[rows], slab.at[rows], slab_sem.at[k])

    for k in range(RB // CHUNK):
        load(k).start()

    barrier = pltpu.get_barrier_semaphore()
    for q in (up, down, across, sibling):
        pl.semaphore_signal(barrier, inc=1, device_id=(q, v), device_id_type=MESH)
    for j in range(1, 16):
        pl.semaphore_signal(barrier, inc=1, device_id=(p, (v + j) % 16), device_id_type=MESH)

    @pl.when(p + v != 0)
    def _():
        pl.semaphore_signal(barrier, inc=1, device_id=(v, (p - v + 16) % 16), device_id_type=MESH)

    lane = lax.broadcasted_iota(jnp.int32, (1, BW), 1)

    def mate_size(block):
        mate, partner = pattern[block], 0
        for other in range(NB):
            partner = jnp.where(mate == other, sizes[other], partner)
        return partner

    mate_sizes = [mate_size(block) for block in range(NB)]

    def live(block, offset):
        return lane < jnp.where(v * SL + offset < sizes[block], mate_sizes[block], 0)

    def hop(f, slot, q, there, index):
        return pltpu.make_async_remote_copy(
            src_ref=gathered.at[f, core, slot], dst_ref=gathered.at[f, core, there],
            send_sem=gat_send.at[f, index], recv_sem=gat_recv.at[f, there], device_id=(q, v), device_id_type=MESH)

    def send_own(f):
        hop(f, 0, up, 1, 0).start()
        hop(f, 0, down, 2, 1).start()
        hop(f, 0, across, 3, 2).start()

    def arrived(f, slot):
        hop(f, slot, sibling, slot, 0).wait_recv()

    def share(f, far, from_core):
        slots = pl.ds(far * 4, 4)
        return pltpu.make_async_remote_copy(
            src_ref=gathered.at[f, from_core, slots], dst_ref=gathered.at[f, from_core, slots],
            send_sem=gat_send.at[f, 7 + far], recv_sem=gat_recv.at[f, 8 + far], device_id=(sibling, v),
            device_id_type=MESH)

    def near(f):
        arrived(f, 1)
        if f == 0:
            hop(f, 1, up, 6, 3).start()
        arrived(f, 2)
        if f == 1:
            hop(f, 2, down, 6, 3).start()
        arrived(f, 3)
        hop(f, 3, up, 4, 4).start()
        hop(f, 3, down, 5, 5).start()
        share(f, 0, core).start()

    def far(f):
        arrived(f, 6)
        hop(f, 6, across, 7, 6).start()
        arrived(f, 4)
        arrived(f, 5)
        arrived(f, 7)
        share(f, 1, core).start()

    def shared(f):
        for k in range(2):
            share(f, k, 1 - core).wait_recv()

    staged[...] = amp[...].astype(F32)

    shift = lax.broadcasted_iota(jnp.int32, (BW, WIN), 1) - lax.broadcasted_iota(jnp.int32, (BW, WIN), 0)
    depth = lax.broadcasted_iota(jnp.int32, (BW, WIN), 0)
    offset = 0
    for block in range(NB):
        inside = depth < mate_sizes[block]
        for odd in range(2):
            chosen = jnp.logical_and(inside, shift == offset + odd * (KP // 2 - (KP - WIN)))
            select[odd, pl.ds(block * BW, BW), :] = jnp.where(chosen, 1.0, 0.0).astype(BF)
        offset = offset + mate_sizes[block]

    def pack(source_ref, rows, put):
        def window(odd, part):
            first, last = REACH[odd][part]
            lanes = pl.ds(first * BW, (last - first) * BW)
            left = source_ref[odd, :, :, lanes].reshape(4 * rows, (last - first) * BW)
            right = select[odd, lanes, pl.ds(part * 256, 256)]
            return lax.dot_general(left, right, (((1,), (0,)), ((), ())), preferred_element_type=F32)

        def save(lane, value):
            value = value.astype(BF)
            for k in range(4):
                put(k, pl.ds(lane, value.shape[1]), value[k * rows:(k + 1) * rows])

        save(0, window(0, 0))
        save(256, window(0, 1))
        low = window(0, 2)
        save(512, low[:, :BW])
        high = window(1, 0)
        save(640, low[:, BW:] + high[:, :BW])
        save(768, high[:, BW:])
        save(896, window(1, 1))
        save(1152, window(1, 2))

    def pack_amplitudes(f):
        def put(k, lanes, value):
            gathered[f, core, 0, k, :, lanes] = value

        pack(few, QS, put)

    for c in range(SL):
        for block in range(NB):
            piece = staged[pl.ds(block * SL + c, QS, stride=NB * SL), :]
            piece = jnp.where(live(block, c), piece, 0.0).astype(BF)
            few[c % 2, c // 2, :, pl.ds(block * BW, BW)] = piece
    pack_amplitudes(0)

    group = lax.broadcasted_iota(jnp.int32, (SL, BW), 1) // SL

    def mix(block, carry):
        tiles = [staged[pl.ds(pl.multiple_of(q * NB * SL + block * SL, SL), SL), :] for q in range(QS)]
        for k in range(4):
            bit = 1 << k
            high = (group // bit) % 2 == 1
            new = list(tiles)
            for q in range(QS):
                if q & bit == 0:
                    new[q] = jnp.where(high, pltpu.roll(tiles[q | bit], SL * bit, 1), tiles[q])
                    new[q | bit] = jnp.where(high, tiles[q | bit], pltpu.roll(tiles[q], BW - SL * bit, 1))
            tiles = new
        for u in range(16):
            mixed[u, pl.ds(pl.multiple_of(block * SL, SL), SL), :] = tiles[u]
        return carry

    lax.fori_loop(0, NB, mix, 0)
    sent[...] = mixed[...].astype(BF)

    g = source[...]
    dy, dh = ((g >> 7) - y) & 3, ((g >> 6) - h) & 1
    slot = jnp.where(dy == 0, dh * 3, jnp.where(dy == 3, 1 + dh * 3, jnp.where(dy == 1, 2 + dh * 3, 6 + dh)))
    place = ((g & 1) * 256 + ((g >> 5) & 1) * 128 + slot * QS + ((g >> 1) & 15)).astype(F32)
    for k in range(4):
        column[pl.ds(k * BW, BW), :] = jnp.broadcast_to(place[k:k + 1, :], (BW, BW)).T.astype(jnp.int32)

    @pl.when(p + v != 0)
    def _():
        pl.semaphore_wait(barrier, 20)

    @pl.when(p + v == 0)
    def _():
        pl.semaphore_wait(barrier, 19)

    send_own(0)
    a2a = []
    for j in range(1, 16):
        u = (v + j) % 16
        copy = pltpu.make_async_remote_copy(
            src_ref=sent.at[u], dst_ref=landed.at[v], send_sem=a2a_send.at[j], recv_sem=a2a_recv.at[j],
            device_id=(p, u), device_id_type=MESH)
        copy.start()
        a2a.append(copy)
    landed[v] = sent[v]

    def relayout(k):
        rows = CHUNK * NB * SL
        w = slab[pl.ds(pl.multiple_of(k * rows, rows), rows), :].reshape(CHUNK, NB, SL, BW)
        for block in range(NB):
            t = jnp.swapaxes(w[:, block], 0, 1)
            for c in range(SL):
                narrow[c % 2, c // 2, :, pl.ds(block * BW, BW)] = t[c]

        def put(j, lanes, value):
            basis[j, pl.ds(pl.multiple_of(k * CHUNK, CHUNK), CHUNK), lanes] = value

        pack(narrow, CHUNK, put)

    def multiply(f):
        rows = pl.ds(f * 256, 256)

        def step(c, carry):
            left = gathered[f, :, :, c].reshape(256, KP)
            part = lax.dot_general(left, basis[c], (((1,), (1,)), ((), ())), preferred_element_type=F32)
            total[rows, :] = total[rows, :] + part
            return carry

        lax.fori_loop(0, 4, step, 0)

    def transposed():
        for copy in a2a:
            copy.wait()
        mixed[...] = landed[...].astype(F32)
        for block in range(NB):
            mate = pattern[block]
            tile = mixed[:, pl.ds(0, SL), :]
            for other in range(1, NB):
                tile = jnp.where(mate == other, mixed[:, pl.ds(other * SL, SL), :], tile)
            turned[...] = tile.reshape(BW, BW).T
            for c in range(SL):
                piece = turned[pl.ds(c, QS, stride=SL), :]
                piece = jnp.where(live(block, c), piece, 0.0).astype(BF)
                few[c % 2, c // 2, :, pl.ds(block * BW, BW)] = piece
        pack_amplitudes(1)
        send_own(1)

    def stage(k, carry):
        load(k).wait()
        relayout(k)

        @pl.when(k == 1)
        def _():
            near(0)

        @pl.when(k == 2)
        def _():
            transposed()

        @pl.when(k == 4)
        def _():
            far(0)

        return carry

    total[...] = jnp.zeros_like(total)
    lax.fori_loop(0, RB // CHUNK, stage, 0)
    shared(0)
    near(1)
    multiply(0)
    far(1)
    shared(1)
    multiply(1)

    for part in range(4):
        rows = pl.ds(part * 128, 128)
        whole = total[rows, :]
        high = whole.astype(BF)
        rest = whole - high.astype(F32)
        middle = rest.astype(BF)
        pieces[0, rows, :] = high
        pieces[1, rows, :] = middle
        pieces[2, rows, :] = (rest - middle.astype(F32)).astype(BF)

    def reorder(which, first, owners):
        takes = []
        for owner in owners:
            rows = pl.ds(pl.multiple_of((owner + p) % 16 * PD, PD), PD)
            takes.append(jnp.concatenate([jnp.where(column[rows, :] == lane + k * BW, 1.0, 0.0) for k in range(4)], axis=1))
        take = jnp.concatenate(takes, axis=0).astype(BF)
        rows = lax.dot_general(take, pieces[0], (((1,), (0,)), ((), ())), preferred_element_type=F32)
        for k in (1, 2):
            rows += lax.dot_general(take, pieces[k], (((1,), (0,)), ((), ())), preferred_element_type=F32)
        for j in range(4):
            ordered[which, first + j] = rows[j * PD:(j + 1) * PD]

    order = [(z + dz) % 8 for dz in FAR + (0,)]
    x_copies = []
    for part in (0, 4):
        reorder(0, part, [u * 2 + 1 - xl for u in order[part:part + 4]])
        for j in (part, part + 2):
            pieces_two = pl.ds(j, 2)
            copy = pltpu.make_async_remote_copy(
                src_ref=ordered.at[0, pieces_two], dst_ref=from_x.at[pieces_two], send_sem=x_send.at[j],
                recv_sem=x_recv.at[j], device_id=(p, z * 2 + 1 - xl), device_id_type=MESH)
            copy.start()
            x_copies.append(copy)
    for part in (0, 4):
        reorder(1, part, [u * 2 + xl for u in order[part:part + 4]])
    z_copies = []
    for j, dz in enumerate(FAR + (0,)):
        owner = ((z + dz) % 8) * 2 + xl
        if j % 2 == 0:
            x_copies[j // 2].wait_recv()
        ordered[1, j] = ordered[1, j] + from_x[j]
        if dz:
            copy = pltpu.make_async_remote_copy(
                src_ref=ordered.at[1, j], dst_ref=from_z.at[j], send_sem=z_send.at[j], recv_sem=z_recv.at[j],
                device_id=(p, owner), device_id_type=MESH)
            copy.start()
            z_copies.append(copy)
    acc = ordered[1, 7]
    for j, copy in enumerate(z_copies):
        copy.wait_recv()
        acc = acc + from_z[j]
    summed[...] = acc

    @pl.when(p + v == 0)
    def _():
        final[...] = summed[...]

    @pl.when(p + v != 0)
    def _():
        copy = pltpu.make_async_remote_copy(
            src_ref=summed, dst_ref=final, send_sem=fin_send, recv_sem=fin_recv, device_id=((p + v) % 16, p),
            device_id_type=MESH)
        copy.start()
        copy.wait()

    for i in range(RD):
        row = v * RD + i
        width = 0
        for block in range(NB):
            here = jnp.where(row // NB < sizes[block], mate_sizes[block], 0)
            width = jnp.where(row % NB == block, here, width)
        lanes = pl.ds(i * BW, BW)
        out[:, lanes] = jnp.where(lane < width, final[:, lanes], 0.0)
    for copy in x_copies + z_copies:
        copy.wait_send()

    for f in range(2):
        for index in range(7):
            hop(f, 0, sibling, 0, index).wait_send()
        for k in range(2):
            share(f, k, core).wait_send()


def on_device(amplitudes, integrals, pattern, block_sizes, pair_source):
    vmem, smem = pl.BlockSpec(memory_space=pltpu.VMEM), pl.BlockSpec(memory_space=pltpu.SMEM)
    dma = pltpu.SemaphoreType.DMA
    result = pl.pallas_call(
        ladder_kernel,
        out_shape=jax.ShapeDtypeStruct((PD, RB), F32),
        in_specs=[vmem, pl.BlockSpec(memory_space=pl.ANY), smem, smem, vmem],
        out_specs=vmem,
        scratch_shapes=[
            pltpu.VMEM((RB * NB * SL, BW), BF),
            pltpu.VMEM((2, 4, CHUNK, LANES), BF),
            pltpu.VMEM((2, LANES, WIN), BF),
            pltpu.VMEM((2, 4, QS, LANES), BF),
            pltpu.VMEM((4, RB, KP), BF),
            pltpu.VMEM((2, 2, 8, 4, QS, KP), BF),
            pltpu.VMEM((512, RB), F32),
            pltpu.VMEM((2, 8, PD, RB), F32),
            pltpu.VMEM((8, PD, RB), F32),
            pltpu.VMEM((7, PD, RB), F32),
            pltpu.VMEM((3, 512, RB), BF),
            pltpu.VMEM((QS * NB * SL, BW), F32),
            pltpu.VMEM((16, NB * SL, BW), F32),
            pltpu.VMEM((16, NB * SL, BW), BF),
            pltpu.VMEM((16, NB * SL, BW), BF),
            pltpu.VMEM((BW, BW), F32),
            pltpu.VMEM((512, BW), jnp.int32),
            pltpu.VMEM((PD, RB), F32),
            pltpu.VMEM((PD, RB), F32),
            dma((RB // CHUNK,)),
            dma((16,)), dma((16,)),
            dma((2, 9)), dma((2, 10)),
            dma((8,)), dma((8,)), dma((7,)), dma((7,)),
            dma, dma,
        ],
        compiler_params=pltpu.CompilerParams(collective_id=0, has_side_effects=True, vmem_limit_bytes=60 * 2**20),
        cost_estimate=pl.CostEstimate(flops=2 * 512 * RB * 8192, bytes_accessed=14 * 2**20, transcendentals=0),
    )(amplitudes.reshape(QS * NB * SL, BW), integrals.reshape(RB * NB * SL, BW), pattern, block_sizes, pair_source.reshape(4, BW))
    return result.reshape(PD, RD, BW)


def solution(mesh):
    return jax.shard_map(
        on_device,
        mesh=mesh,
        in_specs=(P("pair", None, "virt", None), P("pair", None, None, "virt", None), P(), P(), P()),
        out_specs=P("pair", "virt", None),
        check_vma=False,
    )
```

time: 107 us -> 90.8 us (0.85)
  Pallas kernels: 103 us -> 89.1 us
  local copies, waits for them, and re-layouts: 3.06 us -> 1.54 us
    pallas_call x1, Pallas kernels: 103 us -> 89.1 us  [on_device(): pl.pallas_call(ladder_kernel, out_shape=jax.ShapeDtypeStruct((PD, RB), F3...]
    reshape x1 -> x0, local copies, waits for them, and re-layouts: 1.52 us -> none  [on_device(): pair_source.reshape(512, 1)]
where the time goes in v3:
time: 90.8 us; the launch traced here: 90.7 us
  Pallas kernels  89.1 us (98%)
  local copies, waits for them, and re-layouts  1.54 us (2%)
    pallas_call x1, Pallas kernels, on_device(): pl.pallas_call(ladder_kernel, out_shape=jax.ShapeDtypeStruct((PD, RB), F3...  89.1 us

profile of v3, /device:TPU:28, one launch (start us, length us, event | category | flops | bytes accessed | tf_op | source)
XLA Modules:
  0.0 90.7 jit_solution(9820679685477912451)
XLA Ops:
  0.0 89.1 %shard_map.55 = f32[32,768]{1,0:T(8,128)} custom-call(bf16[1024,128]{1,0:T(8,128)(2,1)} %bitcast.9, bf16[49152,128]{1,0:T(8,128)(2,1)} %bitcast.8, s32[8]{0:T(128)} %pattern.1, s32[8]{0:T(128)} %sizes.1, s32[4,128]{1,0:T(4,128)} %bitcast.10), custom_call_target="tpu_custom_call" | custom-call | flops 6442450944 | bytes 14680064 | tf_op jit(solution)/shard_map/pallas_call | solution.py:357
  89.2 1.5 %copy_bitcast_fusion = f32[32,6,128]{2,0,1:T(8,128)} fusion(f32[32,768]{1,0:T(8,128)} %shard_map.55), kind=kLoop, calls=%fused_computation | loop fusion | bytes 196608 | tf_op jit(solution)/shard_map/reshape | solution.py:391

commit v4 on v3

--- a/solution.py
+++ b/solution.py
@@ -18,11 +18,15 @@
 WIN = 768
 REACH = (((0, 6), (2, 8), (4, 8)), ((0, 6), (0, 8), (2, 8)))
 FAR = (4, 3, 5, 2, 6, 1, 7)
-
-
-def ladder_kernel(amp, integrals, pattern, sizes, source, out, slab, narrow, select, few, basis, gathered, total, ordered, from_x, from_z, pieces,
-                  staged, mixed, sent, landed, turned, column, summed, final,
+COLS = ((0, 512), (512, 256))
+
+
+def ladder_kernel(amp, integrals, pattern, sizes, source, out, slab, narrow, select, few, basis, gathered, total, ordered_a, ordered_b, from_x_a, from_x_b, from_z_a,
+                  from_z_b, pieces,
+                  staged, mixed, sent, landed, turned, column, summed_a, summed_b, final_a, final_b,
                   slab_sem, a2a_send, a2a_recv, gat_send, gat_recv, x_send, x_recv, z_send, z_recv, fin_send, fin_recv):
+    ordered, from_x, from_z = (ordered_a, ordered_b), (from_x_a, from_x_b), (from_z_a, from_z_b)
+    summed, final = (summed_a, summed_b), (final_a, final_b)
     p, v = lax.axis_index("pair"), lax.axis_index("virt")
     y, h, core = p // 4, (p // 2) % 2, p % 2
     z, xl = v // 2, v % 2
@@ -278,70 +282,85 @@
         pieces[1, rows, :] = middle
         pieces[2, rows, :] = (rest - middle.astype(F32)).astype(BF)
 
-    def reorder(which, first, owners):
+    order = [(z + dz) % 8 for dz in FAR + (0,)]
+
+    def reorder(group, which, first, count):
+        start, width = COLS[group]
         takes = []
-        for owner in owners:
+        for u in order[first:first + count]:
+            owner = u * 2 + (xl if which else 1 - xl)
             rows = pl.ds(pl.multiple_of((owner + p) % 16 * PD, PD), PD)
             takes.append(jnp.concatenate([jnp.where(column[rows, :] == lane + k * BW, 1.0, 0.0) for k in range(4)], axis=1))
         take = jnp.concatenate(takes, axis=0).astype(BF)
-        rows = lax.dot_general(take, pieces[0], (((1,), (0,)), ((), ())), preferred_element_type=F32)
+        lanes = pl.ds(start, width)
+        rows = lax.dot_general(take, pieces[0, :, lanes], (((1,), (0,)), ((), ())), preferred_element_type=F32)
         for k in (1, 2):
-            rows += lax.dot_general(take, pieces[k], (((1,), (0,)), ((), ())), preferred_element_type=F32)
-        for j in range(4):
-            ordered[which, first + j] = rows[j * PD:(j + 1) * PD]
-
-    order = [(z + dz) % 8 for dz in FAR + (0,)]
-    x_copies = []
-    for part in (0, 4):
-        reorder(0, part, [u * 2 + 1 - xl for u in order[part:part + 4]])
-        for j in (part, part + 2):
-            pieces_two = pl.ds(j, 2)
-            copy = pltpu.make_async_remote_copy(
-                src_ref=ordered.at[0, pieces_two], dst_ref=from_x.at[pieces_two], send_sem=x_send.at[j],
-                recv_sem=x_recv.at[j], device_id=(p, z * 2 + 1 - xl), device_id_type=MESH)
-            copy.start()
-            x_copies.append(copy)
-    for part in (0, 4):
-        reorder(1, part, [u * 2 + xl for u in order[part:part + 4]])
-    z_copies = []
-    for j, dz in enumerate(FAR + (0,)):
-        owner = ((z + dz) % 8) * 2 + xl
-        if j % 2 == 0:
-            x_copies[j // 2].wait_recv()
-        ordered[1, j] = ordered[1, j] + from_x[j]
-        if dz:
-            copy = pltpu.make_async_remote_copy(
-                src_ref=ordered.at[1, j], dst_ref=from_z.at[j], send_sem=z_send.at[j], recv_sem=z_recv.at[j],
-                device_id=(p, owner), device_id_type=MESH)
-            copy.start()
-            z_copies.append(copy)
-    acc = ordered[1, 7]
-    for j, copy in enumerate(z_copies):
-        copy.wait_recv()
-        acc = acc + from_z[j]
-    summed[...] = acc
-
-    @pl.when(p + v == 0)
-    def _():
-        final[...] = summed[...]
-
-    @pl.when(p + v != 0)
-    def _():
-        copy = pltpu.make_async_remote_copy(
-            src_ref=summed, dst_ref=final, send_sem=fin_send, recv_sem=fin_recv, device_id=((p + v) % 16, p),
-            device_id_type=MESH)
-        copy.start()
-        copy.wait()
-
-    for i in range(RD):
-        row = v * RD + i
-        width = 0
-        for block in range(NB):
-            here = jnp.where(row // NB < sizes[block], mate_sizes[block], 0)
-            width = jnp.where(row % NB == block, here, width)
-        lanes = pl.ds(i * BW, BW)
-        out[:, lanes] = jnp.where(lane < width, final[:, lanes], 0.0)
-    for copy in x_copies + z_copies:
+            rows += lax.dot_general(take, pieces[k, :, lanes], (((1,), (0,)), ((), ())), preferred_element_type=F32)
+        for j in range(count):
+            ordered[group][which, first + j] = rows[j * PD:(j + 1) * PD]
+
+    x_copies = [[], []]
+    for group, count in ((0, 2), (1, 4)):
+        for first in range(0, 8, 4):
+            reorder(group, 0, first, 4)
+            for j in range(first, first + 4, count):
+                some = pl.ds(j, count)
+                copy = pltpu.make_async_remote_copy(
+                    src_ref=ordered[group].at[0, some], dst_ref=from_x[group].at[some], send_sem=x_send.at[group, j],
+                    recv_sem=x_recv.at[group, j], device_id=(p, z * 2 + 1 - xl), device_id_type=MESH)
+                copy.start()
+                x_copies[group].append(copy)
+    for group in range(2):
+        for first in range(0, 8, 4):
+            reorder(group, 1, first, 4)
+    z_copies = [[], []]
+    for group, count in ((0, 2), (1, 4)):
+        for j, dz in enumerate(FAR + (0,)):
+            if j % count == 0:
+                x_copies[group][j // count].wait_recv()
+            ordered[group][1, j] = ordered[group][1, j] + from_x[group][j]
+            if dz:
+                copy = pltpu.make_async_remote_copy(
+                    src_ref=ordered[group].at[1, j], dst_ref=from_z[group].at[j], send_sem=z_send.at[group, j],
+                    recv_sem=z_recv.at[group, j], device_id=(p, order[j] * 2 + xl), device_id_type=MESH)
+                copy.start()
+                z_copies[group].append(copy)
+
+    def last(group):
+        return pltpu.make_async_remote_copy(
+            src_ref=summed[group], dst_ref=final[group], send_sem=fin_send.at[group], recv_sem=fin_recv.at[group],
+            device_id=((p + v) % 16, p), device_id_type=MESH)
+
+    for group in range(2):
+        acc = ordered[group][1, 7]
+        for j, copy in enumerate(z_copies[group]):
+            copy.wait_recv()
+            acc = acc + from_z[group][j]
+        summed[group][...] = acc
+
+        @pl.when(p + v != 0)
+        def _():
+            last(group).start()
+
+        @pl.when(p + v == 0)
+        def _():
+            final[group][...] = summed[group][...]
+
+    for group in range(2):
+        @pl.when(p + v != 0)
+        def _():
+            last(group).wait()
+
+        start, width = COLS[group]
+        for i in range(start // BW, (start + width) // BW):
+            row = v * RD + i
+            live_width = 0
+            for block in range(NB):
+                here = jnp.where(row // NB < sizes[block], mate_sizes[block], 0)
+                live_width = jnp.where(row % NB == block, here, live_width)
+            piece = final[group][:, pl.ds(i * BW - start, BW)]
+            out[:, pl.ds(i * BW, BW)] = jnp.where(lane < live_width, piece, 0.0)
+    for copy in x_copies[0] + x_copies[1] + z_copies[0] + z_copies[1]:
         copy.wait_send()
 
     for f in range(2):
@@ -367,9 +386,9 @@
             pltpu.VMEM((4, RB, KP), BF),
             pltpu.VMEM((2, 2, 8, 4, QS, KP), BF),
             pltpu.VMEM((512, RB), F32),
-            pltpu.VMEM((2, 8, PD, RB), F32),
-            pltpu.VMEM((8, PD, RB), F32),
-            pltpu.VMEM((7, PD, RB), F32),
+            *[pltpu.VMEM((2, 8, PD, width), F32) for _, width in COLS],
+            *[pltpu.VMEM((8, PD, width), F32) for _, width in COLS],
+            *[pltpu.VMEM((7, PD, width), F32) for _, width in COLS],
             pltpu.VMEM((3, 512, RB), BF),
             pltpu.VMEM((QS * NB * SL, BW), F32),
             pltpu.VMEM((16, NB * SL, BW), F32),
@@ -377,13 +396,13 @@
             pltpu.VMEM((16, NB * SL, BW), BF),
             pltpu.VMEM((BW, BW), F32),
             pltpu.VMEM((512, BW), jnp.int32),
-            pltpu.VMEM((PD, RB), F32),
-            pltpu.VMEM((PD, RB), F32),
+            *[pltpu.VMEM((PD, width), F32) for _, width in COLS],
+            *[pltpu.VMEM((PD, width), F32) for _, width in COLS],
             dma((RB // CHUNK,)),
             dma((16,)), dma((16,)),
             dma((2, 9)), dma((2, 10)),
-            dma((8,)), dma((8,)), dma((7,)), dma((7,)),
-            dma, dma,
+            dma((2, 8)), dma((2, 8)), dma((2, 7)), dma((2, 7)),
+            dma((2,)), dma((2,)),
         ],
         compiler_params=pltpu.CompilerParams(collective_id=0, has_side_effects=True, vmem_limit_bytes=60 * 2**20),
         cost_estimate=pl.CostEstimate(flops=2 * 512 * RB * 8192, bytes_accessed=14 * 2**20, transcendentals=0),

time: 90.8 us -> 87.1 us (0.959)
  Pallas kernels: 89.1 us -> 84.6 us
    pallas_call x1, Pallas kernels: 89.1 us -> 84.6 us  [on_device(): pl.pallas_call(ladder_kernel, out_shape=jax.ShapeDtypeStruct((PD, RB), F3...]
where the time goes in v4:
time: 87.1 us; the launch traced here: 86.2 us
  Pallas kernels  84.6 us (97%)
  local copies, waits for them, and re-layouts  1.54 us (2%)
    pallas_call x1, Pallas kernels, on_device(): pl.pallas_call(ladder_kernel, out_shape=jax.ShapeDtypeStruct((PD, RB), F3...  84.6 us

profile of v4, /device:TPU:28, one launch (start us, length us, event | category | flops | bytes accessed | tf_op | source)
XLA Modules:
  0.0 86.2 jit_solution(11387987564821764979)
XLA Ops:
  0.0 84.6 %shard_map.55 = f32[32,768]{1,0:T(8,128)} custom-call(bf16[1024,128]{1,0:T(8,128)(2,1)} %bitcast.9, bf16[49152,128]{1,0:T(8,128)(2,1)} %bitcast.8, s32[8]{0:T(128)} %pattern.1, s32[8]{0:T(128)} %sizes.1, s32[4,128]{1,0:T(4,128)} %bitcast.10), custom_call_target="tpu_custom_call" | custom-call | flops 6442450944 | bytes 14680064 | tf_op jit(solution)/shard_map/pallas_call | solution.py:376
  84.6 1.5 %copy_bitcast_fusion = f32[32,6,128]{2,0,1:T(8,128)} fusion(f32[32,768]{1,0:T(8,128)} %shard_map.55), kind=kLoop, calls=%fused_computation | loop fusion | bytes 196608 | tf_op jit(solution)/shard_map/reshape | solution.py:410

commit v5 on v4

--- a/solution.py
+++ b/solution.py
@@ -18,7 +18,7 @@
 WIN = 768
 REACH = (((0, 6), (2, 8), (4, 8)), ((0, 6), (0, 8), (2, 8)))
 FAR = (4, 3, 5, 2, 6, 1, 7)
-COLS = ((0, 512), (512, 256))
+COLS, BATCH = ((0, 512), (512, 256)), ((0, 2), (1, 4))
 
 
 def ladder_kernel(amp, integrals, pattern, sizes, source, out, slab, narrow, select, few, basis, gathered, total, ordered_a, ordered_b, from_x_a, from_x_b, from_z_a,
@@ -86,21 +86,29 @@
             send_sem=gat_send.at[f, 7 + far], recv_sem=gat_recv.at[f, 8 + far], device_id=(sibling, v),
             device_id_type=MESH)
 
+    def bend(f, half, slot, q):
+        part = pl.ds(half * 2, 2)
+        return pltpu.make_async_remote_copy(
+            src_ref=gathered.at[f, core, slot, part], dst_ref=gathered.at[f, core, 6, part],
+            send_sem=gat_send.at[f, 3 + half * 6], recv_sem=gat_recv.at[f, 6 - half * 6], device_id=(q, v),
+            device_id_type=MESH)
+
     def near(f):
         arrived(f, 1)
-        if f == 0:
-            hop(f, 1, up, 6, 3).start()
+        bend(f, 0, 1, up).start()
         arrived(f, 2)
-        if f == 1:
-            hop(f, 2, down, 6, 3).start()
+        bend(f, 1, 2, down).start()
         arrived(f, 3)
         hop(f, 3, up, 4, 4).start()
         hop(f, 3, down, 5, 5).start()
         share(f, 0, core).start()
 
+    def onward(f):
+        for half in range(2):
+            bend(f, half, 6, sibling).wait_recv()
+        hop(f, 6, across, 7, 6).start()
+
     def far(f):
-        arrived(f, 6)
-        hop(f, 6, across, 7, 6).start()
         arrived(f, 4)
         arrived(f, 5)
         arrived(f, 7)
@@ -217,13 +225,14 @@
 
         pack(narrow, CHUNK, put)
 
-    def multiply(f):
-        rows = pl.ds(f * 256, 256)
+    def multiply(f, start, width):
+        rows, lanes = pl.ds(f * 256, 256), pl.ds(start, width)
 
         def step(c, carry):
             left = gathered[f, :, :, c].reshape(256, KP)
-            part = lax.dot_general(left, basis[c], (((1,), (1,)), ((), ())), preferred_element_type=F32)
-            total[rows, :] = total[rows, :] + part
+            right = basis[c, lanes, :]
+            part = lax.dot_general(left, right, (((1,), (1,)), ((), ())), preferred_element_type=F32)
+            total[rows, lanes] = total[rows, lanes] + part
             return carry
 
         lax.fori_loop(0, 4, step, 0)
@@ -259,6 +268,7 @@
 
         @pl.when(k == 4)
         def _():
+            onward(0)
             far(0)
 
         return carry
@@ -267,20 +277,23 @@
     lax.fori_loop(0, RB // CHUNK, stage, 0)
     shared(0)
     near(1)
-    multiply(0)
+    multiply(0, 0, 512)
+    onward(1)
+    multiply(0, 512, 256)
     far(1)
     shared(1)
-    multiply(1)
-
-    for part in range(4):
-        rows = pl.ds(part * 128, 128)
-        whole = total[rows, :]
-        high = whole.astype(BF)
-        rest = whole - high.astype(F32)
-        middle = rest.astype(BF)
-        pieces[0, rows, :] = high
-        pieces[1, rows, :] = middle
-        pieces[2, rows, :] = (rest - middle.astype(F32)).astype(BF)
+
+    def split(start, width):
+        lanes = pl.ds(start, width)
+        for part in range(4):
+            rows = pl.ds(part * 128, 128)
+            whole = total[rows, lanes]
+            high = whole.astype(BF)
+            rest = whole - high.astype(F32)
+            middle = rest.astype(BF)
+            pieces[0, rows, lanes] = high
+            pieces[1, rows, lanes] = middle
+            pieces[2, rows, lanes] = (rest - middle.astype(F32)).astype(BF)
 
     order = [(z + dz) % 8 for dz in FAR + (0,)]
 
@@ -299,8 +312,10 @@
         for j in range(count):
             ordered[group][which, first + j] = rows[j * PD:(j + 1) * PD]
 
-    x_copies = [[], []]
-    for group, count in ((0, 2), (1, 4)):
+    x_copies = [[] for _ in COLS]
+    for group, count in BATCH:
+        multiply(1, *COLS[group])
+        split(*COLS[group])
         for first in range(0, 8, 4):
             reorder(group, 0, first, 4)
             for j in range(first, first + 4, count):
@@ -310,11 +325,11 @@
                     recv_sem=x_recv.at[group, j], device_id=(p, z * 2 + 1 - xl), device_id_type=MESH)
                 copy.start()
                 x_copies[group].append(copy)
-    for group in range(2):
+    for group in range(len(COLS)):
         for first in range(0, 8, 4):
             reorder(group, 1, first, 4)
-    z_copies = [[], []]
-    for group, count in ((0, 2), (1, 4)):
+    z_copies = [[] for _ in COLS]
+    for group, count in BATCH:
         for j, dz in enumerate(FAR + (0,)):
             if j % count == 0:
                 x_copies[group][j // count].wait_recv()
@@ -331,7 +346,7 @@
             src_ref=summed[group], dst_ref=final[group], send_sem=fin_send.at[group], recv_sem=fin_recv.at[group],
             device_id=((p + v) % 16, p), device_id_type=MESH)
 
-    for group in range(2):
+    for group in range(len(COLS)):
         acc = ordered[group][1, 7]
         for j, copy in enumerate(z_copies[group]):
             copy.wait_recv()
@@ -346,7 +361,7 @@
         def _():
             final[group][...] = summed[group][...]
 
-    for group in range(2):
+    for group in range(len(COLS)):
         @pl.when(p + v != 0)
         def _():
             last(group).wait()
@@ -360,12 +375,14 @@
                 live_width = jnp.where(row % NB == block, here, live_width)
             piece = final[group][:, pl.ds(i * BW - start, BW)]
             out[:, pl.ds(i * BW, BW)] = jnp.where(lane < live_width, piece, 0.0)
-    for copy in x_copies[0] + x_copies[1] + z_copies[0] + z_copies[1]:
+    for copy in sum(x_copies + z_copies, []):
         copy.wait_send()
 
     for f in range(2):
-        for index in range(7):
+        for index in (0, 1, 2, 4, 5, 6):
             hop(f, 0, sibling, 0, index).wait_send()
+        for half in range(2):
+            bend(f, half, 6, sibling).wait_send()
         for k in range(2):
             share(f, k, core).wait_send()
 
@@ -400,7 +417,7 @@
             *[pltpu.VMEM((PD, width), F32) for _, width in COLS],
             dma((RB // CHUNK,)),
             dma((16,)), dma((16,)),
-            dma((2, 9)), dma((2, 10)),
+            dma((2, 10)), dma((2, 10)),
             dma((2, 8)), dma((2, 8)), dma((2, 7)), dma((2, 7)),
             dma((2,)), dma((2,)),
         ],

time: 87.1 us -> 85.7 us (0.984)
  Pallas kernels: 84.6 us -> 82.9 us
    pallas_call x1, Pallas kernels: 84.6 us -> 82.9 us  [on_device(): pl.pallas_call(ladder_kernel, out_shape=jax.ShapeDtypeStruct((PD, RB), F3...]
where the time goes in v5:
time: 85.7 us; the launch traced here: 84.4 us
  Pallas kernels  82.9 us (97%)
  local copies, waits for them, and re-layouts  1.54 us (2%)
    pallas_call x1, Pallas kernels, on_device(): pl.pallas_call(ladder_kernel, out_shape=jax.ShapeDtypeStruct((PD, RB), F3...  82.9 us

profile of v5, /device:TPU:28, one launch (start us, length us, event | category | flops | bytes accessed | tf_op | source)
XLA Modules:
  0.0 84.4 jit_solution(4676231340057811321)
XLA Ops:
  0.0 82.9 %shard_map.55 = f32[32,768]{1,0:T(8,128)} custom-call(bf16[1024,128]{1,0:T(8,128)(2,1)} %bitcast.9, bf16[49152,128]{1,0:T(8,128)(2,1)} %bitcast.8, s32[8]{0:T(128)} %pattern.1, s32[8]{0:T(128)} %sizes.1, s32[4,128]{1,0:T(4,128)} %bitcast.10), custom_call_target="tpu_custom_call" | custom-call | flops 6442450944 | bytes 14680064 | tf_op jit(solution)/shard_map/pallas_call | solution.py:393
  82.9 1.5 %copy_bitcast_fusion = f32[32,6,128]{2,0,1:T(8,128)} fusion(f32[32,768]{1,0:T(8,128)} %shard_map.55), kind=kLoop, calls=%fused_computation | loop fusion | bytes 196608 | tf_op jit(solution)/shard_map/reshape | solution.py:427

commit v6 on v5

--- a/solution.py
+++ b/solution.py
@@ -374,7 +374,7 @@
                 here = jnp.where(row // NB < sizes[block], mate_sizes[block], 0)
                 live_width = jnp.where(row % NB == block, here, live_width)
             piece = final[group][:, pl.ds(i * BW - start, BW)]
-            out[:, pl.ds(i * BW, BW)] = jnp.where(lane < live_width, piece, 0.0)
+            out[i] = jnp.where(lane < live_width, piece, 0.0)
     for copy in sum(x_copies + z_copies, []):
         copy.wait_send()
 
@@ -392,7 +392,7 @@
     dma = pltpu.SemaphoreType.DMA
     result = pl.pallas_call(
         ladder_kernel,
-        out_shape=jax.ShapeDtypeStruct((PD, RB), F32),
+        out_shape=jax.ShapeDtypeStruct((RD, PD, BW), F32),
         in_specs=[vmem, pl.BlockSpec(memory_space=pl.ANY), smem, smem, vmem],
         out_specs=vmem,
         scratch_shapes=[
@@ -424,7 +424,7 @@
         compiler_params=pltpu.CompilerParams(collective_id=0, has_side_effects=True, vmem_limit_bytes=60 * 2**20),
         cost_estimate=pl.CostEstimate(flops=2 * 512 * RB * 8192, bytes_accessed=14 * 2**20, transcendentals=0),
     )(amplitudes.reshape(QS * NB * SL, BW), integrals.reshape(RB * NB * SL, BW), pattern, block_sizes, pair_source.reshape(4, BW))
-    return result.reshape(PD, RD, BW)
+    return result.transpose(1, 0, 2)
 
 
 def solution(mesh):

time: 85.7 us -> 85.7 us (level)
    reshape x1 -> x0, local copies, waits for them, and re-layouts: 1.54 us -> none  [on_device(): return result.reshape(PD, RD, BW)]
    unnamed x0 -> x1, local copies, waits for them, and re-layouts: none -> 1.54 us
where the time goes in v6:
time: 85.7 us; the launch traced here: 84.4 us
  Pallas kernels  82.9 us (97%)
  local copies, waits for them, and re-layouts  1.54 us (2%)
    pallas_call x1, Pallas kernels, on_device(): pl.pallas_call(ladder_kernel, out_shape=jax.ShapeDtypeStruct((RD, PD, BW)...  82.9 us

profile of v6, /device:TPU:28, one launch (start us, length us, event | category | flops | bytes accessed | tf_op | source)
XLA Modules:
  0.0 84.4 jit_solution(12181930639467734200)
XLA Ops:
  0.0 82.9 %shard_map.55 = f32[6,32,128]{2,1,0:T(8,128)} custom-call(bf16[1024,128]{1,0:T(8,128)(2,1)} %bitcast.6, bf16[49152,128]{1,0:T(8,128)(2,1)} %bitcast.5, s32[8]{0:T(128)} %pattern.1, s32[8]{0:T(128)} %sizes.1, s32[4,128]{1,0:T(4,128)} %bitcast.7), custom_call_target="tpu_custom_call" | custom-call | flops 6442450944 | bytes 14680064 | tf_op jit(solution)/shard_map/pallas_call | solution.py:393
  82.9 1.5 %copy.7 = f32[32,6,128]{2,0,1:T(8,128)} copy(f32[32,6,128]{2,0,1:T(8,128)} %bitcast.4) | data formatting | bytes 196608
